TPU v7x, 32 devices: a whole 2x2x4 slice. The times are simulated.
32 devices in a mesh: groups: 2 (over y), mp: 4 (over x, core), embed: 4 (over z).
Axes of the slice: x: 2, y: 2, z: 4, core: 2. Of those that a mesh axis runs over, the one named last changes fastest.
Arguments:
- x_rows: bfloat16 [64, 18432], P(('groups', 'mp'), 'embed'), parts along dimension 0, may hold values from -6 to 6
- joined_weight: bfloat16 [18432, 12800], P('embed', 'mp'), may hold values from -0.046875 to 0.046875
- cache_keys: bfloat16 [64, 512, 256], P(('groups', 'mp', 'embed')), parts along dimension 0, may hold values from -384 to 384
- cache_values: bfloat16 [64, 512, 256], P(('groups', 'mp', 'embed')), parts along dimension 0, may hold values from -6 to 6
- lengths: int32 [64], P(('groups', 'mp', 'embed')), parts along dimension 0, may hold values from 1 to 512, as said below
- out_weight: bfloat16 [12288, 18432], P('mp', 'embed'), may hold values from -0.0546875 to 0.0546875
Outputs:
- layer_out: bfloat16 [64, 18432], P(('groups', 'mp'), 'embed'), parts along dimension 0
There are 2 independent parts, one for each index of `groups`. A program takes and returns all parts, laid end to end along the dimension named above; an argument that names none is the same for every part. Nothing has to cross between parts.
Inputs may be any that keep to these rules, and one draw needn't show every extreme that they name: `lengths`: some row of every draw has exactly 512 valid positions.
All inputs are finite; a program needn't handle non-finite values.
Results may differ from a plain program's by a relative error of at most 0.012.
The roundings to bfloat16 on the way count: a program that leaves them out, or rounds other values in their place, can miss the bound.
Values may be sent and summed in bfloat16 or wider, within the bound.
A program may use at most 128 MiB of HBM per device.

v0:
```python
import math

import jax
import jax.numpy as jnp
from jax import lax
from jax.sharding import PartitionSpec as P


def body(x_rows, joined_weight, cache_keys, cache_values, lengths, out_weight):
    mp_count = lax.axis_size("mp")
    embed_count = lax.axis_size("embed")
    rows_here = cache_keys.shape[0]
    cache_len = cache_keys.shape[1]
    head_dim = cache_keys.shape[2]
    local_columns = joined_weight.shape[1]
    partial_sums = jnp.dot(
        lax.all_gather(x_rows, "mp", axis=0, tiled=True),
        joined_weight,
        preferred_element_type=jnp.float32,
    )
    shaped = partial_sums.reshape(mp_count, embed_count, rows_here, local_columns)
    summed = lax.psum_scatter(shaped, "embed", scatter_dimension=1, tiled=True).astype(jnp.bfloat16)
    arrived = lax.all_to_all(summed, "mp", split_axis=0, concat_axis=3, tiled=True)
    projected = arrived.reshape(rows_here, local_columns * mp_count)
    query_width = projected.shape[1] - 2 * head_dim
    head_count = query_width // head_dim
    queries = projected[:, :query_width].reshape(rows_here, head_count, head_dim)
    new_key = projected[:, query_width : query_width + head_dim]
    new_value = projected[:, query_width + head_dim :]
    score_scale = 1.0 / math.sqrt(head_dim)
    scores = (
        jnp.einsum("rhd,rld->rhl", queries, cache_keys, preferred_element_type=jnp.float32)
        * score_scale
    )
    new_score = (
        jnp.einsum("rhd,rd->rh", queries, new_key, preferred_element_type=jnp.float32) * score_scale
    )
    visible = jnp.arange(cache_len, dtype=jnp.int32)[None, None, :] < lengths[:, None, None]
    scores = jnp.where(visible, scores, -1e30)
    highest = jnp.maximum(jnp.max(scores, axis=-1), new_score)
    expo = jnp.where(visible, jnp.exp(scores - highest[..., None]), 0.0)
    new_expo = jnp.exp(new_score - highest)
    denominator = jnp.sum(expo, axis=-1) + new_expo
    weights = (expo / denominator[..., None]).astype(jnp.bfloat16)
    new_weight = (new_expo / denominator).astype(jnp.bfloat16)
    attended = jnp.einsum("rhl,rld->rhd", weights, cache_values, preferred_element_type=jnp.float32)
    attended = (
        attended
        + new_weight.astype(jnp.float32)[..., None] * new_value.astype(jnp.float32)[:, None, :]
    )
    attended = attended.astype(jnp.bfloat16).reshape(rows_here, mp_count, query_width // mp_count)
    returned = lax.all_to_all(attended, "mp", split_axis=1, concat_axis=0, tiled=True)
    returned = returned.reshape(mp_count, 1, rows_here, query_width // mp_count)
    partial_out = jnp.einsum(
        "ikrw,wd->ikrd",
        lax.all_gather(returned, "embed", axis=1, tiled=True),
        out_weight,
        preferred_element_type=jnp.float32,
    )
    partial_out = partial_out.reshape(mp_count * embed_count * rows_here, out_weight.shape[1])
    result = lax.psum_scatter(partial_out, "mp", scatter_dimension=0, tiled=True)
    return result.astype(jnp.bfloat16)


def solution(mesh):
    return jax.shard_map(
        body,
        mesh=mesh,
        in_specs=(
            P(("groups", "mp"), "embed"),
            P("embed", "mp"),
            P(("groups", "mp", "embed"), None, None),
            P(("groups", "mp", "embed"), None, None),
            P(("groups", "mp", "embed")),
            P("mp", "embed"),
        ),
        out_specs=P(("groups", "mp"), "embed"),
        check_vma=False,
    )
```

profile of v0, /device:TPU:0, one launch (start us, length us, event | category | flops | bytes accessed | tf_op | source)
XLA Modules:
  0.0 126.1 jit_solution(4797440305507389968)
XLA Ops:
  6.5 0.0 copy-start
  6.5 0.0 copy-start.3
  6.5 0.0 copy-start.1
  6.5 0.0 copy-start.2
  6.5 7.7 %all_gather.6 = bf16[32,4608]{1,0:T(8,128)(2,1)S(1)} all-gather(bf16[8,4608]{1,0:T(8,128)(2,1)} %param.6), channel_id=1, replica_groups=mesh['groups'=2,'mp'=4,'embed'=4] {'mp'}, dimensions={0}, use_global_device_ids=true | all-gather | bytes 368640 | tf_op jit(solution)/shard_map/all_gather | solution.py:17
  14.3 12.1 %fusion.20 = f32[32,3200]{1,0:T(8,128)S(1)} fusion(bf16[32,4608]{1,0:T(8,128)(2,1)S(1)} %all_gather.6, bf16[4608,3200]{1,0:T(8,128)(2,1)} %param.7), kind=kOutput, calls=%fused_computation.31 | convolution fusion | flops 943718400 | bytes 30195712 | tf_op jit(solution)/shard_map/dot_general | solution.py:16
  26.4 0.2 reshape.45
  26.6 0.1 copy.14
  26.7 27.7 %all-reduce.2 = bf16[4,4,2,3200]{3,0,2,1:T(4,128)(2,1)S(1)} all-reduce(f32[4,4,2,3200]{3,0,2,1:T(4,128)S(1)} %copy.14), channel_id=3, replica_groups=mesh['groups'=2,'mp'=4,'embed'=4] {'embed'}, use_global_device_ids=true, to_apply=%region_0.0.clone | all-reduce | flops 102400 | bytes 614400
  54.4 0.0 copy-done.3
  54.4 0.6 dynamic-slice
  55.0 0.7 dynamic-slice_convert_fusion
  55.7 0.7 copy.15
  56.3 3.3 %all-to-all-start = ((bf16[4,1,2,3200]{3,2,1,0:T(2,128)(2,1)}), bf16[4,1,2,3200]{3,2,1,0:T(2,128)(2,1)S(1)}, u32[]{:S(2)}, u32[]{:S(2)}) async-start(bf16[4,1,2,3200]{3,2,1,0:T(2,128)(2,1)} %copy.15), calls=%async_computation | async-start | bytes 102400 | tf_op jit(solution)/shard_map/all_to_all | solution.py:23
  59.6 0.0 reduce-scatter.2.cloned.1.call-start
  59.7 0.0 copy-done.1
  59.7 0.1 iota_compare_fusion
  59.8 3.9 %all-to-all-done = bf16[4,1,2,3200]{3,2,1,0:T(2,128)(2,1)S(1)} async-done(((bf16[4,1,2,3200]{3,2,1,0:T(2,128)(2,1)}), bf16[4,1,2,3200]{3,2,1,0:T(2,128)(2,1)S(1)}, u32[]{:S(2)}, u32[]{:S(2)}) %all-to-all-start) | async-done | bytes 51232 | tf_op jit(solution)/shard_map/all_to_all | solution.py:23
  63.7 0.1 fusion.10
  63.8 0.0 copy-done
  63.8 0.4 fusion.19
  64.2 0.2 fusion.5
  64.4 0.0 copy-done.2
  64.4 0.3 fusion.3
  64.7 6.4 %all_to_all.30 = bf16[2,4,3072]{2,0,1:T(2,128)(2,1)S(1)} all-to-all(bf16[2,4,3072]{2,0,1:T(2,128)(2,1)S(1)} %copy.16), channel_id=1, replica_groups=mesh['groups'=2,'mp'=4,'embed'=4] {'mp'}, dimensions={1} | all-to-all | bytes 98304 | tf_op jit(solution)/shard_map/all_to_all | solution.py:52
  71.1 13.9 %all-gather = bf16[4,8,1,3072]{3,0,2,1:T(4,128)(2,1)S(1)} all-gather(bf16[4,2,1,3072]{3,0,2,1:T(4,128)(2,1)S(1)} %copy.17), channel_id=2, replica_groups=mesh['groups'=2,'mp'=4,'embed'=4] {'embed'}, dimensions={1}, use_global_device_ids=true | all-gather | bytes 245760 | tf_op jit(solution)/shard_map/all_gather | solution.py:56
  85.0 11.9 %fusion = f32[4,4,2,4608]{3,2,1,0:T(2,128)S(1)} fusion(bf16[3072,4608]{1,0:T(8,128)(2,1)} %param.11, bf16[4,4,2,3072]{3,0,2,1:T(4,128)(2,1)S(1)} %bitcast.31), kind=kOutput, calls=%fused_computation | convolution fusion | flops 905969664 | bytes 29097984 | tf_op jit(solution)/shard_map/ikrw,wd->ikrd/dot_general | solution.py:54
  96.9 1.2 reshape.50
  98.2 0.0 reduce-scatter.2.cloned.1.call-update
  98.2 19.6 %reduce-scatter.2.cloned.1.call-done = f32[8,4608]{1,0:T(8,128)} async-done(((f32[32,4608]{1,0:T(8,128)}), f32[8,4608]{1,0:T(8,128)}) %reduce-scatter.2.cloned.1.call-update) | async-done | bytes 147472 | tf_op jit(solution)/shard_map/reduce_scatter | solution.py:61
  117.7 1.6 %convert_element_type.27 = bf16[8,4608]{1,0:T(8,128)(2,1)} convert(f32[8,4608]{1,0:T(8,128)} %reduce-scatter.2.cloned.1.call-done) | non-fusion elementwise | flops 36864 | bytes 221184 | tf_op jit(solution)/shard_map/convert_element_type | solution.py:62
  (7 shorter events, 0.1 us)
Async XLA Ops:
  6.5 57.3 %copy-start = (bf16[2,512,256]{2,1,0:T(8,128)(2,1)S(1)}, bf16[2,512,256]{2,1,0:T(8,128)(2,1)}, u32[]{:S(2)}) copy-start(bf16[2,512,256]{2,1,0:T(8,128)(2,1)} %param.8) | copy-start | bytes 1572868
  6.5 47.9 %copy-start.3 = (u32[32]{0:T(128)S(1)}, u32[32]{0:T(128)}, u32[]{:S(2)}) copy-start(u32[32]{0:T(128)} %constant.14) | copy-start | bytes 388
  6.5 53.1 %copy-start.1 = (s32[2]{0:T(128)S(1)}, s32[2]{0:T(128)}, u32[]{:S(2)}) copy-start(s32[2]{0:T(128)} %param.10) | copy-start | bytes 28
  6.5 57.8 %copy-start.2 = (bf16[2,512,256]{2,1,0:T(8,128)(2,1)S(1)}, bf16[2,512,256]{2,1,0:T(8,128)(2,1)}, u32[]{:S(2)}) copy-start(bf16[2,512,256]{2,1,0:T(8,128)(2,1)} %param.9) | copy-start | bytes 1572868
  56.3 7.3 %all-to-all-start = ((bf16[4,1,2,3200]{3,2,1,0:T(2,128)(2,1)}), bf16[4,1,2,3200]{3,2,1,0:T(2,128)(2,1)S(1)}, u32[]{:S(2)}, u32[]{:S(2)}) async-start(bf16[4,1,2,3200]{3,2,1,0:T(2,128)(2,1)} %copy.15), calls=%async_computation | async-start | bytes 102400 | tf_op jit(solution)/shard_map/all_to_all | solution.py:23
  59.6 58.1 %reduce-scatter.2.cloned.1.call-start = ((), (), s32[]{:S(2)}) async-start(), calls=%async_computation.3 | async-start | bytes 737280 | tf_op jit(solution)/shard_map/reduce_scatter | solution.py:61
Sparse Core Ops, SparseCore 0:
  98.3 19.4 reduce-scatter.1
where the time goes:
time: 126 us
  blocking collectives  55.7 us (44%)
  matrix products  24.7 us (20%)
  waiting for transfers between devices  23.5 us (19%)
  between operations  13.5 us (11%)
  local copies, waits for them, and re-layouts  3.61 us (3%)
  starting transfers between devices  3.32 us (3%)
  other arithmetic  1.84 us (1%)
    unnamed x1, blocking collectives  27.7 us
    reduce_scatter x1, waiting for transfers between devices, body(): lax.psum_scatter(partial_out, 'mp', scatter_dimension=0, tiled=True)  19.6 us
    all_gather x1, blocking collectives, body(): lax.all_gather(returned, 'embed', axis=1, tiled=True)  13.9 us
    dot_general x1, matrix products, body(): jnp.dot(lax.all_gather(x_rows, 'mp', axis=0, tiled=True), joined_weight,...  12.1 us
    dot_general x1, matrix products, body(): jnp.einsum('ikrw,wd->ikrd', lax.all_gather(returned, 'embed', axis=1, til...  11.9 us
    all_gather x1, blocking collectives, body(): lax.all_gather(x_rows, 'mp', axis=0, tiled=True)  7.71 us
    all_to_all x1, blocking collectives, body(): lax.all_to_all(attended, 'mp', split_axis=1, concat_axis=0, tiled=True)  6.39 us
    all_to_all x1, waiting for transfers between devices, body(): lax.all_to_all(summed, 'mp', split_axis=0, concat_axis=3, tiled=True)  3.88 us
  transfers between devices with their start and end apart: 2, of which 2 were waited for; matrix products, arithmetic and copies ran while one was open for 0% of the time, Pallas kernels for 0%

commit v1 on v0

--- a/solution.py
+++ b/solution.py
@@ -1,12 +1,412 @@
+import functools
 import math
 
 import jax
 import jax.numpy as jnp
 from jax import lax
+from jax.experimental import pallas as pl
+from jax.experimental.pallas import tpu as pltpu
 from jax.sharding import PartitionSpec as P
 
 
-def body(x_rows, joined_weight, cache_keys, cache_values, lengths, out_weight):
+LANES = 128
+JOINED_TILE = 512
+OUT_TILE = 256
+F32 = jnp.float32
+BF16 = jnp.bfloat16
+VMEM_BYTES = 63 * 1024 * 1024
+
+
+def fused_kernel(
+    sizes,
+    lengths_ref,
+    x_ref,
+    wj_ref,
+    ck_ref,
+    cv_ref,
+    wo_ref,
+    out_ref,
+    x_in,
+    x_pack,
+    x_all,
+    lhs,
+    wj,
+    wo,
+    keys,
+    values,
+    partial,
+    partial_in,
+    rows_out,
+    rows_in,
+    query,
+    att,
+    att_rows,
+    att_out,
+    att_in,
+    att_f32,
+    att_lhs,
+    product,
+    out_send,
+    out_in,
+    load_sem,
+    wj_sem,
+    wo_sem,
+    x_ssem,
+    x_rsem,
+    b_ssem,
+    b_rsem,
+    c_ssem,
+    c_rsem,
+    d_ssem,
+    d_rsem,
+    f_ssem,
+    f_rsem,
+):
+    mp, em, heads, dh, cache_len = sizes
+    me = lax.axis_index("mp")
+    my = lax.axis_index("embed")
+    count = mp * em
+    own = me * em + my
+    rows_x, width = x_ref.shape
+    half = width // 2
+    columns = wj_ref.shape[1]
+    chunks = columns // LANES
+    full = columns // JOINED_TILE
+    rest = columns - full * JOINED_TILE
+    out_half = out_ref.shape[1] // 2
+    pairs = out_half // OUT_TILE
+    heads_here = heads // mp
+
+    def remote(src, dst, ssem, rsem, p, q):
+        return pltpu.make_async_remote_copy(
+            src_ref=src,
+            dst_ref=dst,
+            send_sem=ssem,
+            recv_sem=rsem,
+            device_id={"mp": p, "embed": q},
+            device_id_type=pl.DeviceIdType.MESH,
+        )
+
+    def tile(j, size=JOINED_TILE):
+        return pl.ds(pl.multiple_of(j * JOINED_TILE, LANES), size)
+
+    def wj_copy(j, size=JOINED_TILE):
+        return pltpu.make_async_copy(wj_ref.at[:, tile(j, size)], wj.at[:, tile(j, size)], wj_sem.at[j])
+
+    def wo_copy(j, side):
+        place = pl.ds(pl.multiple_of(side * out_half + j * OUT_TILE, LANES), OUT_TILE)
+        return pltpu.make_async_copy(wo_ref.at[:, place], wo.at[:, place], wo_sem.at[side, j])
+
+    x_load = pltpu.make_async_copy(x_ref, x_in, load_sem.at[0])
+    x_load.start()
+
+    @pl.loop(0, full)
+    def _(j):
+        wj_copy(j).start()
+
+    if rest:
+        wj_copy(full, rest).start()
+    key_load = pltpu.make_async_copy(ck_ref, keys, load_sem.at[1])
+    value_load = pltpu.make_async_copy(cv_ref, values, load_sem.at[2])
+    key_load.start()
+    value_load.start()
+
+    barrier = pltpu.get_barrier_semaphore()
+
+    @pl.loop(1, count)
+    def _(d):
+        t = lax.rem(own + d, count)
+        pl.semaphore_signal(
+            barrier,
+            inc=1,
+            device_id={"mp": t // em, "embed": lax.rem(t, em)},
+            device_id_type=pl.DeviceIdType.MESH,
+        )
+
+    x_load.wait()
+    x32 = x_in[...].astype(F32)
+    x_pack[...] = jnp.concatenate([x32[:, :half], x32[:, half:]], axis=0).astype(BF16)
+    pl.semaphore_wait(barrier, count - 1)
+
+    def x_slot(p):
+        return x_all.at[pl.ds(pl.multiple_of(p * 2 * rows_x, 2 * rows_x), 2 * rows_x), :]
+
+    for d in range(1, mp):
+        p = lax.rem(me + d, mp)
+        remote(x_pack, x_slot(me), x_ssem.at[d], x_rsem.at[me], p, my).start()
+    x_slot(me)[...] = x_pack[...]
+    for d in range(1, mp):
+        p = lax.rem(me + d, mp)
+        remote(x_pack, x_slot(p), x_ssem.at[d], x_rsem.at[p], p, my).wait_recv()
+
+    total = mp * rows_x
+    row = lax.broadcasted_iota(jnp.int32, (total, 2 * total), 0)
+    col = lax.broadcasted_iota(jnp.int32, (total, 2 * total), 1)
+    wanted = (lax.rem(row, 2 * mp) // 2) * (2 * rows_x) + (row // (2 * mp)) * 2 + lax.rem(row, 2)
+    for side in range(2):
+        pick = jnp.where(col == wanted + side * rows_x, 1.0, 0.0).astype(BF16)
+        lhs[:, side * half : (side + 1) * half] = jnp.dot(
+            pick, x_all[...], preferred_element_type=F32
+        ).astype(BF16)
+
+    def b_rows(q):
+        return pl.ds(pl.multiple_of(q * 2 * mp, 2 * mp), 2 * mp)
+
+    def project(j, size):
+        wj_copy(j, size).wait()
+        partial[:, tile(j, size)] = jnp.dot(lhs[...], wj[:, tile(j, size)], preferred_element_type=F32)
+        for d in range(1, em):
+            q = lax.rem(my + d, em)
+            remote(
+                partial.at[b_rows(q), tile(j, size)],
+                partial_in.at[my, :, tile(j, size)],
+                b_ssem.at[d, j],
+                b_rsem.at[my, j],
+                me,
+                q,
+            ).start()
+
+    @pl.loop(0, full)
+    def _(j):
+        project(j, JOINED_TILE)
+
+        @pl.when(j < pairs)
+        def _():
+            wo_copy(j, 0).start()
+            wo_copy(j, 1).start()
+
+    if rest:
+        project(full, rest)
+
+    @pl.loop(min(full, pairs), pairs)
+    def _(j):
+        wo_copy(j, 0).start()
+        wo_copy(j, 1).start()
+
+    stride = rows_out.shape[0] // (2 * mp)
+
+    def collect(j, size):
+        for d in range(1, em):
+            q = lax.rem(my + d, em)
+            remote(
+                partial.at[b_rows(q), tile(j, size)],
+                partial_in.at[q, :, tile(j, size)],
+                b_ssem.at[d, j],
+                b_rsem.at[q, j],
+                me,
+                q,
+            ).wait()
+        total_here = partial[b_rows(my), tile(j, size)]
+        for d in range(1, em):
+            total_here += partial_in[lax.rem(my + d, em), :, tile(j, size)]
+        total_here = total_here.astype(BF16).astype(F32)
+        for c in range(size // LANES):
+            rows_out[pl.ds(j * (JOINED_TILE // LANES) + c, 2 * mp, stride=stride), :] = total_here[
+                :, c * LANES : (c + 1) * LANES
+            ]
+
+    for j in range(full):
+        collect(j, JOINED_TILE)
+    if rest:
+        collect(full, rest)
+
+    def c_rows(p):
+        return pl.ds(pl.multiple_of(p * 2 * stride, 2 * stride), 2 * stride)
+
+    for d in range(1, mp):
+        p = lax.rem(me + d, mp)
+        remote(rows_out.at[c_rows(p), :], rows_in.at[me], c_ssem.at[d], c_rsem.at[me], p, my).start()
+    rows_in[me] = rows_out[c_rows(me), :]
+    for d in range(1, mp):
+        p = lax.rem(me + d, mp)
+        remote(rows_out.at[c_rows(p), :], rows_in.at[p], c_ssem.at[d], c_rsem.at[p], p, my).wait()
+
+    key_load.wait()
+    value_load.wait()
+    scale = 1.0 / math.sqrt(dh)
+    base = query.shape[0] // 2
+    for r in range(2):
+        for s in range(mp):
+            query[pl.ds(r * base + s * chunks, stride), :] = rows_in[s, r * stride : (r + 1) * stride, :]
+    for r in range(2):
+        at = r * base
+        q32 = jnp.concatenate(
+            [query[pl.ds(at, heads, stride=2), :], query[pl.ds(at + 1, heads, stride=2), :]], axis=1
+        )
+        end = at + 2 * heads
+        new_key = jnp.concatenate([query[end : end + 1, :], query[end + 1 : end + 2, :]], axis=1)
+        new_value = jnp.concatenate([query[end + 2 : end + 3, :], query[end + 3 : end + 4, :]], axis=1)
+        scores = (
+            lax.dot_general(
+                q32.astype(BF16), keys[r], (((1,), (1,)), ((), ())), preferred_element_type=F32
+            )
+            * scale
+        )
+        new_score = jnp.sum(q32 * new_key, axis=1, keepdims=True) * scale
+        visible = lax.broadcasted_iota(jnp.int32, (heads, cache_len), 1) < lengths_ref[r]
+        scores = jnp.where(visible, scores, -1e30)
+        highest = jnp.maximum(jnp.max(scores, axis=1, keepdims=True), new_score)
+        expo = jnp.where(visible, jnp.exp(scores - highest), 0.0)
+        new_expo = jnp.exp(new_score - highest)
+        denominator = jnp.sum(expo, axis=1, keepdims=True) + new_expo
+        weights = (expo / denominator).astype(BF16)
+        new_weight = (new_expo / denominator).astype(BF16).astype(F32)
+        attended = jnp.dot(weights, values[r], preferred_element_type=F32) + new_weight * new_value
+        for side in range(2):
+            att[...] = attended[:, side * LANES : (side + 1) * LANES]
+            for p in range(mp):
+                first = (p * 2 + r) * 2 * heads_here + side * heads_here
+                att_rows[pl.ds(first, heads_here), :] = att[pl.ds(p * heads_here, heads_here), :]
+    att_out[...] = att_rows[...].astype(BF16)
+
+    block = 4 * heads_here
+
+    def d_rows(t):
+        return pl.ds(pl.multiple_of(t * block, block), block)
+
+    def d_copy(d, t_slot, s_slot):
+        t = lax.rem(own + d, count)
+        p, q = t // em, lax.rem(t, em)
+        return remote(
+            att_out.at[d_rows(p), :],
+            att_in.at[d_rows(t_slot), :],
+            d_ssem.at[d],
+            d_rsem.at[s_slot],
+            p,
+            q,
+        )
+
+    @pl.loop(1, count)
+    def _(d):
+        d_copy(d, own, own).start()
+
+    att_in[d_rows(own), :] = att_out[d_rows(me), :]
+
+    @pl.loop(1, count)
+    def _(d):
+        t = lax.rem(own + d, count)
+        d_copy(d, t, t).wait()
+
+    att_f32[...] = att_in[...].astype(F32)
+    for h in range(heads_here):
+        for side in range(2):
+            place = (2 * h + side) * LANES
+            att_lhs[:, place : place + LANES] = att_f32[
+                pl.ds(side * heads_here + h, 2 * count, stride=2 * heads_here), :
+            ].astype(BF16)
+
+    def f_rows(p):
+        return pl.ds(pl.multiple_of(p * rows_x, rows_x), rows_x)
+
+    def f_copy(d, j, p, slot):
+        place = pl.ds(pl.multiple_of(j * OUT_TILE, LANES), OUT_TILE)
+        return remote(
+            out_send.at[p, :, place], out_in.at[slot, :, place], f_ssem.at[d, j], f_rsem.at[slot, j], p, my
+        )
+
+    @pl.loop(0, pairs)
+    def _(j):
+        here = [
+            pl.ds(pl.multiple_of(side * out_half + j * OUT_TILE, LANES), OUT_TILE) for side in range(2)
+        ]
+        for side in range(2):
+            wo_copy(j, side).wait()
+            product[:, here[side]] = jnp.dot(
+                att_lhs[...], wo[:, here[side]], preferred_element_type=F32
+            )
+        for d in range(1, mp):
+            p = lax.rem(me + d, mp)
+            out_send[p, :, pl.ds(pl.multiple_of(j * OUT_TILE, LANES), OUT_TILE)] = jnp.concatenate(
+                [product[f_rows(p), here[0]], product[f_rows(p), here[1]]], axis=0
+            ).astype(BF16)
+            f_copy(d, j, p, me).start()
+
+    @pl.loop(0, pairs)
+    def _(j):
+        place = pl.ds(pl.multiple_of(j * OUT_TILE, LANES), OUT_TILE)
+        here = [
+            pl.ds(pl.multiple_of(side * out_half + j * OUT_TILE, LANES), OUT_TILE) for side in range(2)
+        ]
+        acc = jnp.concatenate([product[f_rows(me), here[0]], product[f_rows(me), here[1]]], axis=0)
+        for d in range(1, mp):
+            p = lax.rem(me + d, mp)
+            f_copy(d, j, p, p).wait()
+            acc += out_in[p, :, place].astype(F32)
+        out_ref[:, here[0]] = acc[:rows_x].astype(BF16)
+        out_ref[:, here[1]] = acc[rows_x:].astype(BF16)
+
+    for d in range(1, mp):
+        p = lax.rem(me + d, mp)
+        remote(x_pack, x_slot(me), x_ssem.at[d], x_rsem.at[me], p, my).wait_send()
+
+
+def fused_body(x_rows, joined_weight, cache_keys, cache_values, lengths, out_weight):
+    mp = lax.axis_size("mp")
+    em = lax.axis_size("embed")
+    rows_x, width = x_rows.shape
+    _, cache_len, dh = cache_keys.shape
+    columns = joined_weight.shape[1]
+    features, out_width = out_weight.shape
+    heads = features * mp // dh
+    chunks = columns // LANES
+    stride = -(-chunks // 8) * 8
+    total = mp * rows_x
+    count = mp * em
+    tiles = -(-columns // JOINED_TILE)
+    pairs = out_width // 2 // OUT_TILE
+    block = 4 * (heads // mp)
+    dma = pltpu.SemaphoreType.DMA
+    scratch = [
+        pltpu.VMEM((rows_x, width), BF16),
+        pltpu.VMEM((2 * rows_x, width // 2), BF16),
+        pltpu.VMEM((2 * total, width // 2), BF16),
+        pltpu.VMEM((total, width), BF16),
+        pltpu.VMEM(joined_weight.shape, BF16),
+        pltpu.VMEM(out_weight.shape, BF16),
+        pltpu.VMEM(cache_keys.shape, BF16),
+        pltpu.VMEM(cache_values.shape, BF16),
+        pltpu.VMEM((total, columns), F32),
+        pltpu.VMEM((em, 2 * mp, columns), F32),
+        pltpu.VMEM((2 * mp * stride, LANES), F32),
+        pltpu.VMEM((mp, 2 * stride, LANES), F32),
+        pltpu.VMEM((2 * (mp * chunks // 8 * 8 + stride), LANES), F32),
+        pltpu.VMEM((heads, LANES), F32),
+        pltpu.VMEM((mp * block, LANES), F32),
+        pltpu.VMEM((mp * block, LANES), BF16),
+        pltpu.VMEM((count * block, LANES), BF16),
+        pltpu.VMEM((count * block, LANES), F32),
+        pltpu.VMEM((total, features), BF16),
+        pltpu.VMEM((total, out_width), F32),
+        pltpu.VMEM((mp, 2 * rows_x, out_width // 2), BF16),
+        pltpu.VMEM((mp, 2 * rows_x, out_width // 2), BF16),
+        dma((3,)),
+        dma((tiles,)),
+        dma((2, pairs)),
+        dma((mp,)),
+        dma((mp,)),
+        dma((em, tiles)),
+        dma((em, tiles)),
+        dma((mp,)),
+        dma((mp,)),
+        dma((count,)),
+        dma((count,)),
+        dma((mp, pairs)),
+        dma((mp, pairs)),
+    ]
+    hbm = pl.BlockSpec(memory_space=pl.ANY)
+    return pl.pallas_call(
+        functools.partial(fused_kernel, (mp, em, heads, dh, cache_len)),
+        out_shape=jax.ShapeDtypeStruct((rows_x, out_width), BF16),
+        in_specs=[pl.BlockSpec(memory_space=pltpu.SMEM)] + [hbm] * 5,
+        out_specs=pl.BlockSpec(memory_space=pltpu.VMEM),
+        scratch_shapes=scratch,
+        compiler_params=pltpu.CompilerParams(
+            collective_id=0, has_side_effects=True, vmem_limit_bytes=VMEM_BYTES
+        ),
+    )(lengths, x_rows, joined_weight, cache_keys, cache_values, out_weight)
+
+
+def plain_body(x_rows, joined_weight, cache_keys, cache_values, lengths, out_weight):
     mp_count = lax.axis_size("mp")
     embed_count = lax.axis_size("embed")
     rows_here = cache_keys.shape[0]
@@ -60,6 +460,31 @@
     partial_out = partial_out.reshape(mp_count * embed_count * rows_here, out_weight.shape[1])
     result = lax.psum_scatter(partial_out, "mp", scatter_dimension=0, tiled=True)
     return result.astype(jnp.bfloat16)
+
+
+def body(x_rows, joined_weight, cache_keys, cache_values, lengths, out_weight):
+    mp = lax.axis_size("mp")
+    em = lax.axis_size("embed")
+    rows_x, width = x_rows.shape
+    rows_here, _, dh = cache_keys.shape
+    columns = joined_weight.shape[1]
+    features, out_width = out_weight.shape
+    held = 2 * (joined_weight.size + out_weight.size + cache_keys.size + cache_values.size)
+    fits = (
+        rows_here == 2
+        and rows_x == 8
+        and em * 2 == rows_x
+        and mp * 2 == 8
+        and dh == 2 * LANES
+        and columns % LANES == 0
+        and width % (2 * LANES) == 0
+        and features % dh == 0
+        and (features // dh) % 4 == 0
+        and out_width % (2 * OUT_TILE) == 0
+        and held < VMEM_BYTES - 6 * 1024 * 1024
+    )
+    chosen = fused_body if fits else plain_body
+    return chosen(x_rows, joined_weight, cache_keys, cache_values, lengths, out_weight)
 
 
 def solution(mesh):

time: 126 us -> 49.9 us (0.40)
  blocking collectives: 55.7 us -> 0 us
  Pallas kernels: 0 us -> 48.2 us
  matrix products: 24.7 us -> 0 us
  waiting for transfers between devices: 23.5 us -> 0 us
  between operations: 13.5 us -> 0.01 us
  starting transfers between devices: 3.32 us -> 0 us
  local copies, waits for them, and re-layouts: 3.61 us -> 1.52 us
  other arithmetic: 1.84 us -> 0 us
    pallas_call x0 -> x1, Pallas kernels: none -> 48.2 us  [fused_body(): pl.pallas_call(functools.partial(fused_kernel, (mp, em, heads, dh, cache_...]
    unnamed x1 -> x0, blocking collectives: 27.7 us -> none
    dot_general x5 -> x0, matrix products: 24.7 us -> none  [the longest x1 12.1 us: body(): jnp.dot(lax.all_gather(x_rows, 'mp', axis=0, tiled=True), joined_weight,...]
    all_gather x2 -> x0, blocking collectives: 21.6 us -> none  [the longest x1 13.9 us: body(): lax.all_gather(returned, 'embed', axis=1, tiled=True)]
    reduce_scatter x1 -> x0, waiting for transfers between devices: 19.6 us -> none  [body(): lax.psum_scatter(partial_out, 'mp', scatter_dimension=0, tiled=True)]
    all_to_all x1 -> x0, blocking collectives: 6.39 us -> none  [body(): lax.all_to_all(attended, 'mp', split_axis=1, concat_axis=0, tiled=True)]
    all_to_all x1 -> x0, waiting for transfers between devices: 3.88 us -> none  [body(): lax.all_to_all(summed, 'mp', split_axis=0, concat_axis=3, tiled=True)]
    all_to_all x1 -> x0, starting transfers between devices: 3.28 us -> none  [body(): lax.all_to_all(summed, 'mp', split_axis=0, concat_axis=3, tiled=True)]
  transfers between devices with their start and end apart: 2 -> 0, of which waited for: 2 -> 0; matrix products, arithmetic and copies ran while one was open for 0% -> 0% of each run, Pallas kernels for 0% -> 0%
where the time goes in v1:
time: 49.9 us; the launch traced here: 49.8 us
  Pallas kernels  48.2 us (97%)
  local copies, waits for them, and re-layouts  1.52 us (3%)
    pallas_call x1, Pallas kernels, fused_body(): pl.pallas_call(functools.partial(fused_kernel, (mp, em, heads, dh, cache_...  48.2 us
    unnamed x1, local copies, waits for them, and re-layouts  1.52 us

profile of v1, /device:TPU:0, one launch (start us, length us, event | category | flops | bytes accessed | tf_op | source)
XLA Modules:
  0.0 49.8 jit_solution(10099619179197217939)
XLA Ops:
  0.0 48.2 %shard_map.64 = bf16[8,4608]{1,0:T(8,128)(2,1)} custom-call(s32[2]{0:T(128)} %lengths_ref.1, bf16[8,4608]{1,0:T(8,128)(2,1)} %x_ref.1, bf16[4608,3200]{1,0:T(8,128)(2,1)} %wj_ref.1, bf16[2,512,256]{2,1,0:T(8,128)(2,1)} %ck_ref.1, bf16[2,512,256]{2,1,0:T(8,128)(2,1)} %cv_ref.1, bf16[3072,4608]{1,0:T(8,128)(2,1)} %wo_ref.1), custom_call_target="tpu_custom_call" | custom-call | tf_op jit(solution)/shard_map/pallas_call | solution.py:397
  48.3 1.5 %copy.8 = bf16[8,4608]{1,0:T(8,128)(2,1)} copy(bf16[8,4608]{1,0:T(8,128)(2,1)} %shard_map.64) | data formatting | bytes 147456

commit v2 on v1

--- a/solution.py
+++ b/solution.py
@@ -11,7 +11,8 @@
 
 LANES = 128
 JOINED_TILE = 512
-OUT_TILE = 256
+OUT_TILE = 768
+GROUP = 4
 F32 = jnp.float32
 BF16 = jnp.bfloat16
 VMEM_BYTES = 63 * 1024 * 1024
@@ -76,6 +77,7 @@
     out_half = out_ref.shape[1] // 2
     pairs = out_half // OUT_TILE
     heads_here = heads // mp
+    groups = heads_here // GROUP
 
     def remote(src, dst, ssem, rsem, p, q):
         return pltpu.make_async_remote_copy(
@@ -113,31 +115,37 @@
 
     barrier = pltpu.get_barrier_semaphore()
 
-    @pl.loop(1, count)
-    def _(d):
-        t = lax.rem(own + d, count)
+    for d in range(1, mp):
         pl.semaphore_signal(
-            barrier,
-            inc=1,
-            device_id={"mp": t // em, "embed": lax.rem(t, em)},
-            device_id_type=pl.DeviceIdType.MESH,
+            barrier, inc=1, device_id={"mp": lax.rem(me + d, mp)}, device_id_type=pl.DeviceIdType.MESH
+        )
+    for d in range(1, em):
+        pl.semaphore_signal(
+            barrier, inc=1, device_id={"embed": lax.rem(my + d, em)}, device_id_type=pl.DeviceIdType.MESH
         )
 
     x_load.wait()
     x32 = x_in[...].astype(F32)
     x_pack[...] = jnp.concatenate([x32[:, :half], x32[:, half:]], axis=0).astype(BF16)
-    pl.semaphore_wait(barrier, count - 1)
+    pl.semaphore_wait(barrier, mp + em - 2)
 
     def x_slot(p):
         return x_all.at[pl.ds(pl.multiple_of(p * 2 * rows_x, 2 * rows_x), 2 * rows_x), :]
 
-    for d in range(1, mp):
-        p = lax.rem(me + d, mp)
-        remote(x_pack, x_slot(me), x_ssem.at[d], x_rsem.at[me], p, my).start()
+    core = lax.rem(me, 2)
+    beside = me + 1 - 2 * core
+    across = lax.rem(me + 2, mp)
+    diagonal = lax.rem(beside + 2, mp)
+    send_across = remote(x_pack, x_slot(me), x_ssem.at[1], x_rsem.at[1], across, my)
+    send_beside = remote(x_pack, x_slot(me), x_ssem.at[0], x_rsem.at[0], beside, my)
+    relay = remote(x_slot(across), x_slot(across), x_ssem.at[2], x_rsem.at[2], beside, my)
+    send_across.start()
+    send_beside.start()
     x_slot(me)[...] = x_pack[...]
-    for d in range(1, mp):
-        p = lax.rem(me + d, mp)
-        remote(x_pack, x_slot(p), x_ssem.at[d], x_rsem.at[p], p, my).wait_recv()
+    remote(x_pack, x_slot(across), x_ssem.at[1], x_rsem.at[1], across, my).wait_recv()
+    relay.start()
+    remote(x_pack, x_slot(beside), x_ssem.at[0], x_rsem.at[0], beside, my).wait_recv()
+    remote(x_pack, x_slot(diagonal), x_ssem.at[2], x_rsem.at[2], beside, my).wait_recv()
 
     total = mp * rows_x
     row = lax.broadcasted_iota(jnp.int32, (total, 2 * total), 0)
@@ -254,46 +262,37 @@
         attended = jnp.dot(weights, values[r], preferred_element_type=F32) + new_weight * new_value
         for side in range(2):
             att[...] = attended[:, side * LANES : (side + 1) * LANES]
-            for p in range(mp):
-                first = (p * 2 + r) * 2 * heads_here + side * heads_here
-                att_rows[pl.ds(first, heads_here), :] = att[pl.ds(p * heads_here, heads_here), :]
+            for g in range(groups):
+                for p in range(mp):
+                    first = ((g * mp + p) * 2 + r) * 2 * GROUP + side * GROUP
+                    att_rows[pl.ds(first, GROUP), :] = att[pl.ds(p * heads_here + g * GROUP, GROUP), :]
     att_out[...] = att_rows[...].astype(BF16)
 
-    block = 4 * heads_here
+    block = 4 * GROUP
 
     def d_rows(t):
         return pl.ds(pl.multiple_of(t * block, block), block)
 
-    def d_copy(d, t_slot, s_slot):
+    def d_copy(g, d, slot):
         t = lax.rem(own + d, count)
         p, q = t // em, lax.rem(t, em)
         return remote(
-            att_out.at[d_rows(p), :],
-            att_in.at[d_rows(t_slot), :],
-            d_ssem.at[d],
-            d_rsem.at[s_slot],
+            att_out.at[d_rows(g * mp + p), :],
+            att_in.at[d_rows(g * count + slot), :],
+            d_ssem.at[g, d],
+            d_rsem.at[g, slot],
             p,
             q,
         )
 
-    @pl.loop(1, count)
-    def _(d):
-        d_copy(d, own, own).start()
-
-    att_in[d_rows(own), :] = att_out[d_rows(me), :]
-
-    @pl.loop(1, count)
-    def _(d):
-        t = lax.rem(own + d, count)
-        d_copy(d, t, t).wait()
-
-    att_f32[...] = att_in[...].astype(F32)
-    for h in range(heads_here):
-        for side in range(2):
-            place = (2 * h + side) * LANES
-            att_lhs[:, place : place + LANES] = att_f32[
-                pl.ds(side * heads_here + h, 2 * count, stride=2 * heads_here), :
-            ].astype(BF16)
+    @pl.loop(0, groups)
+    def _(g):
+        @pl.loop(1, count)
+        def _(d):
+            d_copy(g, d, own).start()
+
+    for g in range(groups):
+        att_in[d_rows(g * count + own), :] = att_out[d_rows(g * mp + me), :]
 
     def f_rows(p):
         return pl.ds(pl.multiple_of(p * rows_x, rows_x), rows_x)
@@ -304,22 +303,42 @@
             out_send.at[p, :, place], out_in.at[slot, :, place], f_ssem.at[d, j], f_rsem.at[slot, j], p, my
         )
 
-    @pl.loop(0, pairs)
-    def _(j):
-        here = [
-            pl.ds(pl.multiple_of(side * out_half + j * OUT_TILE, LANES), OUT_TILE) for side in range(2)
-        ]
-        for side in range(2):
-            wo_copy(j, side).wait()
-            product[:, here[side]] = jnp.dot(
-                att_lhs[...], wo[:, here[side]], preferred_element_type=F32
-            )
-        for d in range(1, mp):
-            p = lax.rem(me + d, mp)
-            out_send[p, :, pl.ds(pl.multiple_of(j * OUT_TILE, LANES), OUT_TILE)] = jnp.concatenate(
-                [product[f_rows(p), here[0]], product[f_rows(p), here[1]]], axis=0
-            ).astype(BF16)
-            f_copy(d, j, p, me).start()
+    for g in range(groups):
+
+        @pl.loop(1, count)
+        def _(d):
+            d_copy(g, d, lax.rem(own + d, count)).wait()
+
+        rows = pl.ds(g * count * block, count * block)
+        att_f32[...] = att_in[rows, :].astype(F32)
+        for h in range(GROUP):
+            for side in range(2):
+                place = (2 * h + side) * LANES
+                att_lhs[:, place : place + LANES] = att_f32[
+                    pl.ds(side * GROUP + h, 2 * count, stride=2 * GROUP), :
+                ].astype(BF16)
+        depth = pl.ds(g * GROUP * dh, GROUP * dh)
+
+        @pl.loop(0, pairs)
+        def _(j):
+            here = [
+                pl.ds(pl.multiple_of(side * out_half + j * OUT_TILE, LANES), OUT_TILE) for side in range(2)
+            ]
+            for side in range(2):
+                if g == 0:
+                    wo_copy(j, side).wait()
+                term = jnp.dot(att_lhs[...], wo[depth, here[side]], preferred_element_type=F32)
+                if g == 0:
+                    product[:, here[side]] = term
+                else:
+                    product[:, here[side]] += term
+            if g == groups - 1:
+                for d in range(1, mp):
+                    p = lax.rem(me + d, mp)
+                    out_send[p, :, pl.ds(pl.multiple_of(j * OUT_TILE, LANES), OUT_TILE)] = jnp.concatenate(
+                        [product[f_rows(p), here[0]], product[f_rows(p), here[1]]], axis=0
+                    ).astype(BF16)
+                    f_copy(d, j, p, me).start()
 
     @pl.loop(0, pairs)
     def _(j):
@@ -335,9 +354,9 @@
         out_ref[:, here[0]] = acc[:rows_x].astype(BF16)
         out_ref[:, here[1]] = acc[rows_x:].astype(BF16)
 
-    for d in range(1, mp):
-        p = lax.rem(me + d, mp)
-        remote(x_pack, x_slot(me), x_ssem.at[d], x_rsem.at[me], p, my).wait_send()
+    send_across.wait_send()
+    send_beside.wait_send()
+    relay.wait_send()
 
 
 def fused_body(x_rows, joined_weight, cache_keys, cache_values, lengths, out_weight):
@@ -374,8 +393,8 @@
         pltpu.VMEM((mp * block, LANES), F32),
         pltpu.VMEM((mp * block, LANES), BF16),
         pltpu.VMEM((count * block, LANES), BF16),
-        pltpu.VMEM((count * block, LANES), F32),
-        pltpu.VMEM((total, features), BF16),
+        pltpu.VMEM((4 * GROUP * count, LANES), F32),
+        pltpu.VMEM((total, GROUP * dh), BF16),
         pltpu.VMEM((total, out_width), F32),
         pltpu.VMEM((mp, 2 * rows_x, out_width // 2), BF16),
         pltpu.VMEM((mp, 2 * rows_x, out_width // 2), BF16),
@@ -388,8 +407,8 @@
         dma((em, tiles)),
         dma((mp,)),
         dma((mp,)),
-        dma((count,)),
-        dma((count,)),
+        dma((heads // mp // GROUP, count)),
+        dma((heads // mp // GROUP, count)),
         dma((mp, pairs)),
         dma((mp, pairs)),
     ]
@@ -479,7 +498,7 @@
         and columns % LANES == 0
         and width % (2 * LANES) == 0
         and features % dh == 0
-        and (features // dh) % 4 == 0
+        and (features // dh) % GROUP == 0
         and out_width % (2 * OUT_TILE) == 0
         and held < VMEM_BYTES - 6 * 1024 * 1024
     )

time: 49.9 us -> 44.8 us (0.90)
  Pallas kernels: 48.2 us -> 43.1 us
    pallas_call x1, Pallas kernels: 48.2 us -> 43.1 us  [fused_body(): pl.pallas_call(functools.partial(fused_kernel, (mp, em, heads, dh, cache_...]
where the time goes in v2:
time: 44.8 us; the launch traced here: 44.6 us
  Pallas kernels  43.1 us (96%)
  local copies, waits for them, and re-layouts  1.52 us (3%)
    pallas_call x1, Pallas kernels, fused_body(): pl.pallas_call(functools.partial(fused_kernel, (mp, em, heads, dh, cache_...  43.1 us
    unnamed x1, local copies, waits for them, and re-layouts  1.52 us

profile of v2, /device:TPU:0, one launch (start us, length us, event | category | flops | bytes accessed | tf_op | source)
XLA Modules:
  0.0 44.6 jit_solution(7648777092769721513)
XLA Ops:
  0.0 43.1 %shard_map.64 = bf16[8,4608]{1,0:T(8,128)(2,1)} custom-call(s32[2]{0:T(128)} %lengths_ref.1, bf16[8,4608]{1,0:T(8,128)(2,1)} %x_ref.1, bf16[4608,3200]{1,0:T(8,128)(2,1)} %wj_ref.1, bf16[2,512,256]{2,1,0:T(8,128)(2,1)} %ck_ref.1, bf16[2,512,256]{2,1,0:T(8,128)(2,1)} %cv_ref.1, bf16[3072,4608]{1,0:T(8,128)(2,1)} %wo_ref.1), custom_call_target="tpu_custom_call" | custom-call | tf_op jit(solution)/shard_map/pallas_call | solution.py:416
  43.1 1.5 %copy.8 = bf16[8,4608]{1,0:T(8,128)(2,1)} copy(bf16[8,4608]{1,0:T(8,128)(2,1)} %shard_map.64) | data formatting | bytes 147456

commit v3 on v2

--- a/solution.py
+++ b/solution.py
@@ -10,8 +10,8 @@
 
 
 LANES = 128
-JOINED_TILE = 512
-OUT_TILE = 768
+JOINED_TILE = 640
+OUT_TILE = 1152
 GROUP = 4
 F32 = jnp.float32
 BF16 = jnp.bfloat16
@@ -333,7 +333,7 @@
                 else:
                     product[:, here[side]] += term
             if g == groups - 1:
-                for d in range(1, mp):
+                for d in (2, 1, 3):
                     p = lax.rem(me + d, mp)
                     out_send[p, :, pl.ds(pl.multiple_of(j * OUT_TILE, LANES), OUT_TILE)] = jnp.concatenate(
                         [product[f_rows(p), here[0]], product[f_rows(p), here[1]]], axis=0

time: 44.8 us -> 44.4 us (level)
  no operation moved by 1% of the time
where the time goes in v3:
time: 44.4 us; the launch traced here: 44.2 us
  Pallas kernels  42.7 us (96%)
  local copies, waits for them, and re-layouts  1.52 us (3%)
    pallas_call x1, Pallas kernels, fused_body(): pl.pallas_call(functools.partial(fused_kernel, (mp, em, heads, dh, cache_...  42.7 us
    unnamed x1, local copies, waits for them, and re-layouts  1.52 us

profile of v3, /device:TPU:0, one launch (start us, length us, event | category | flops | bytes accessed | tf_op | source)
XLA Modules:
  0.0 44.2 jit_solution(8062779289637648454)
XLA Ops:
  0.0 42.7 %shard_map.64 = bf16[8,4608]{1,0:T(8,128)(2,1)} custom-call(s32[2]{0:T(128)} %lengths_ref.1, bf16[8,4608]{1,0:T(8,128)(2,1)} %x_ref.1, bf16[4608,3200]{1,0:T(8,128)(2,1)} %wj_ref.1, bf16[2,512,256]{2,1,0:T(8,128)(2,1)} %ck_ref.1, bf16[2,512,256]{2,1,0:T(8,128)(2,1)} %cv_ref.1, bf16[3072,4608]{1,0:T(8,128)(2,1)} %wo_ref.1), custom_call_target="tpu_custom_call" | custom-call | tf_op jit(solution)/shard_map/pallas_call | solution.py:416
  42.7 1.5 %copy.8 = bf16[8,4608]{1,0:T(8,128)(2,1)} copy(bf16[8,4608]{1,0:T(8,128)(2,1)} %shard_map.64) | data formatting | bytes 147456
